TPU v7x, 32 devices: a whole 2x2x4 slice. The times are simulated.
32 devices in a mesh: grp: 2 (over x), blk: 16 (over z, y, core).
Axes of the slice: x: 2, y: 2, z: 4, core: 2. Of those that a mesh axis runs over, the one named last changes fastest.
Arguments:
- vertex_embed: float32 [12288, 256], P(('grp', 'blk')), may hold values from -1.8 to 1.8
- context_embed: float32 [12288, 256], P(('grp', 'blk')), may hold values from -1.8 to 1.8
- counts: int32 [4, 12288, 384], P(None, ('grp', 'blk')), may hold values from 0 to 7
- negatives: int32 [4, 5, 12288], P(None, None, ('grp', 'blk')), may hold values from 0 to 383
- masks: int32 [4, 96, 3], P(None, ('grp', 'blk')), may hold values 0 or 1
Outputs:
- vertex_final: float32 [12288, 256], P(('grp', 'blk'))
- context_final: float32 [12288, 256], P(('grp', 'blk'))
All inputs are finite; a program needn't handle non-finite values. No bound on the sum of `masks` on one device may be relied on, other than what follows from the above.
Results may differ from a plain program's by a relative error of at most 0.0003.
Values sent between devices are 32-bit elements; how exact they have to be, the bound alone decides.
A program may use at most 64 MiB of HBM per device.

v0:
```python
import math

import jax
import jax.numpy as jnp
from jax import lax
from jax.sharding import PartitionSpec as P

ROUNDS = 2
ROUND_PASSES = 2


def passed_along(value, axis, steps):
    count = lax.axis_size(axis)
    pairs = [(source, (source + steps) % count) for source in range(count)]
    return lax.ppermute(value, axis, pairs)


def from_partner(value, axis, stride):
    return lax.ppermute(value, axis, [(i, i ^ 1 << stride) for i in range(lax.axis_size(axis))])


def one_pass(vert, ctx, cnt, neg_rows, tile_mask):
    highest = lax.Precision.HIGHEST
    rows = vert.shape[0]
    tiles = tile_mask.shape[0]
    tile = rows // tiles
    eta = 0.25 / math.sqrt(rows)
    columns = lax.broadcasted_iota(jnp.int32, (1, rows), 1)
    scores = jnp.einsum("iw,jw->ij", vert, ctx, precision=highest)
    sig = jax.nn.sigmoid(scores)
    negcount = jnp.zeros((rows, rows), jnp.float32)
    for sample in range(neg_rows.shape[0]):
        negcount = negcount + (neg_rows[sample][:, None] == columns).astype(jnp.float32)
    coef = cnt.astype(jnp.float32) * (1.0 - sig) - negcount * sig
    gate = tile_mask.astype(jnp.float32)[:, None, :, None]
    coef = (coef.reshape(tiles, tile, tiles, tile) * gate).reshape(rows, rows)
    new_ctx = ctx + eta * jnp.einsum("ij,iw->jw", coef, vert, precision=highest)
    new_vert = vert + eta * jnp.dot(coef, ctx, precision=highest)
    moved = passed_along(new_ctx, "blk", 1)
    return (new_vert, moved)


def on_device(vertex_embed, context_embed, counts, negatives, masks):
    vert = vertex_embed
    ctx = context_embed
    for rnd in range(ROUNDS):
        if rnd > 0:
            vert = from_partner(vert, "grp", 0)
        for step in range(ROUND_PASSES):
            index = rnd * ROUND_PASSES + step
            vert, ctx = one_pass(vert, ctx, counts[index], negatives[index], masks[index])
    return (vert, ctx)


def solution(mesh):
    placed = (
        P(("grp", "blk"), None),
        P(("grp", "blk"), None),
        P(None, ("grp", "blk"), None),
        P(None, None, ("grp", "blk")),
        P(None, ("grp", "blk"), None),
    )
    return jax.shard_map(
        on_device,
        mesh=mesh,
        in_specs=placed,
        out_specs=(P(("grp", "blk"), None), P(("grp", "blk"), None)),
        check_vma=False,
    )
```

profile of v0, /device:TPU:0, one launch (start us, length us, event | category | flops | bytes accessed | tf_op | source)
XLA Modules:
  0.0 58.3 jit_solution(3936864782095175161)
XLA Ops:
  0.6 1.0 %slice_reduce_fusion.4 = (s32[384]{0:T(512)S(1)}, s32[384]{0:T(512)S(1)}, s32[384]{0:T(512)S(1)}, s32[384]{0:T(512)S(1)}, s32[384]{0:T(512)S(1)}, /*index=5*/s32...) fusion(s32[4,5,384]{2,0,1:T(4,128)} %param.8), kind=kLoop, calls=%fused_computation.73 | loop fusion | bytes 58368 | tf_op jit(solution)/shard_map/slice | solution.py:33
  1.7 0.8 %slice_convert_fusion = (f32[1,3,3]{2,0,1:T(1,128)S(1)}, f32[1,3,3]{2,0,1:T(1,128)S(1)}, f32[1,3,3]{2,0,1:T(1,128)S(1)}, f32[1,3,3]{2,0,1:T(1,128)S(1)}) fusion(s32[4,3,3]{2,0,1:T(4,128)} %param.9), kind=kLoop, calls=%fused_computation.68 | loop fusion | flops 36 | bytes 288 | tf_op jit(solution)/shard_map/convert_element_type | solution.py:35
  2.5 0.2 mul.94
  2.7 0.0 copy-start
  2.7 0.0 copy-start.1
  2.7 2.4 %bitcast_multiply_fusion.3 = f32[384,384]{1,0:T(8,128)S(1)} fusion(f32[48,8,3,128]{3,2,1,0:T(4,128)S(1)} %bitcast.72, f32[384,256]{1,0:T(8,128)} %param.5, f32[384,256]{1,0:T(8,128)} %param.6, s32[4,384,384]{2,1,0:T(8,128)} %param.7, s32[384]{0:T(512)S(1)} %get-tuple-element.15, s32[384]{0:T(512)S(1)} %get-tuple-element.16, s32[384]{0:T(512)S(1)} %get-tuple-element.17, ...), kind=kOutput, calls=%fused_computation.35 | convolution fusion | flops 456376320 | bytes 2563584 | tf_op jit(solution)/shard_map/iw,jw->ij/dot_general | solution.py:29
  5.1 0.0 copy-done
  5.1 0.0 copy-done.1
  5.1 0.0 copy-start.2
  5.2 1.1 %fusion.18 = f32[384,256]{1,0:T(8,128)S(1)} fusion(f32[384,256]{1,0:T(8,128)S(1)} %copy-done.1, f32[384,384]{1,0:T(8,128)S(1)} %bitcast_multiply_fusion.3, f32[384,256]{1,0:T(8,128)S(1)} %copy-done), kind=kOutput, calls=%fused_computation.29 | convolution fusion | flops 453181440 | bytes 1769472 | tf_op jit(solution)/shard_map/ij,iw->jw/dot_general | solution.py:37
  6.3 0.5 collective-permute-start
  6.8 0.8 %fusion.19 = f32[384,256]{1,0:T(8,128)S(1)} fusion(f32[384,256]{1,0:T(8,128)S(1)} %copy-done, f32[384,384]{1,0:T(8,128)S(1)} %bitcast_multiply_fusion.3, f32[384,256]{1,0:T(8,128)S(1)} %copy-done.1), kind=kOutput, calls=%fused_computation.31 | convolution fusion | flops 453181440 | bytes 1769472 | tf_op jit(solution)/shard_map/dot_general | solution.py:38
  7.6 9.7 %collective-permute-done = f32[384,256]{1,0:T(8,128)S(1)} collective-permute-done((f32[384,256]{1,0:T(8,128)S(1)}, f32[384,256]{1,0:T(8,128)S(1)}, u32[]{:S(2)}, u32[]{:S(2)}) %collective-permute-start) | collective-permute-done | bytes 393248 | tf_op jit(solution)/shard_map/ppermute | solution.py:15
  17.3 0.2 mul.101
  17.4 0.0 copy-done.2
  17.4 1.7 %bitcast_multiply_fusion.2 = f32[384,384]{1,0:T(8,128)S(1)} fusion(f32[48,8,3,128]{3,2,1,0:T(4,128)S(1)} %bitcast.73, f32[384,256]{1,0:T(8,128)S(1)} %fusion.19, f32[384,256]{1,0:T(8,128)S(1)} %collective-permute-done, s32[4,384,384]{2,1,0:T(8,128)S(1)} %copy-done.2, s32[384]{0:T(512)S(1)} %get-tuple-element.10, s32[384]{0:T(512)S(1)} %get-tuple-element.11, ...), kind=kOutput, calls=%fused_computation.34 | convolution fusion | flops 456376320 | bytes 2563584 | tf_op jit(solution)/shard_map/iw,jw->ij/dot_general | solution.py:29
  19.1 1.1 %fusion.16 = f32[384,256]{1,0:T(8,128)S(1)} fusion(f32[384,256]{1,0:T(8,128)S(1)} %collective-permute-done, f32[384,384]{1,0:T(8,128)S(1)} %bitcast_multiply_fusion.2, f32[384,256]{1,0:T(8,128)S(1)} %fusion.19), kind=kOutput, calls=%fused_computation.25 | convolution fusion | flops 453181440 | bytes 1769472 | tf_op jit(solution)/shard_map/ij,iw->jw/dot_general | solution.py:37
  20.3 0.1 collective-permute-start.2
  20.4 0.8 %fusion.17 = f32[384,256]{1,0:T(8,128)S(1)} fusion(f32[384,256]{1,0:T(8,128)S(1)} %fusion.19, f32[384,384]{1,0:T(8,128)S(1)} %bitcast_multiply_fusion.2, f32[384,256]{1,0:T(8,128)S(1)} %collective-permute-done), kind=kOutput, calls=%fused_computation.27 | convolution fusion | flops 453181440 | bytes 1769472 | tf_op jit(solution)/shard_map/dot_general | solution.py:38
  21.2 2.0 %collective-permute-start.1 = (f32[384,256]{1,0:T(8,128)S(1)}, f32[384,256]{1,0:T(8,128)S(1)}, u32[]{:S(2)}, u32[]{:S(2)}) collective-permute-start(f32[384,256]{1,0:T(8,128)S(1)} %fusion.17), channel_id=1, source_target_pairs={{0,16},{16,0},{1,17},{17,1},{2,18},{18,2},{3,19},{19,3},{4,20},{20... | collective-permute-start | bytes 1179656 | tf_op jit(solution)/shard_map/ppermute | solution.py:19
  23.2 7.1 %collective-permute-done.2 = f32[384,256]{1,0:T(8,128)S(1)} collective-permute-done((f32[384,256]{1,0:T(8,128)S(1)}, f32[384,256]{1,0:T(8,128)S(1)}, u32[]{:S(2)}, u32[]{:S(2)}) %collective-permute-start.2) | collective-permute-done | bytes 393248 | tf_op jit(solution)/shard_map/ppermute | solution.py:15
  30.2 1.4 %collective-permute-done.1 = f32[384,256]{1,0:T(8,128)S(1)} collective-permute-done((f32[384,256]{1,0:T(8,128)S(1)}, f32[384,256]{1,0:T(8,128)S(1)}, u32[]{:S(2)}, u32[]{:S(2)}) %collective-permute-start.1) | collective-permute-done | bytes 393248 | tf_op jit(solution)/shard_map/ppermute | solution.py:19
  31.6 0.2 mul.108
  31.8 1.7 %bitcast_multiply_fusion.1 = f32[384,384]{1,0:T(8,128)S(1)} fusion(f32[48,8,3,128]{3,2,1,0:T(4,128)S(1)} %bitcast.74, f32[384,256]{1,0:T(8,128)S(1)} %collective-permute-done.1, f32[384,256]{1,0:T(8,128)S(1)} %collective-permute-done.2, s32[4,384,384]{2,1,0:T(8,128)S(1)} %copy-done.2, s32[384]{0:T(512)S(1)} %get-tuple-element.5, ...), kind=kOutput, calls=%fused_computation.33 | convolution fusion | flops 456376320 | bytes 2563584 | tf_op jit(solution)/shard_map/iw,jw->ij/dot_general | solution.py:29
  33.5 1.1 %fusion.14 = f32[384,256]{1,0:T(8,128)S(1)} fusion(f32[384,256]{1,0:T(8,128)S(1)} %collective-permute-done.2, f32[384,384]{1,0:T(8,128)S(1)} %bitcast_multiply_fusion.1, f32[384,256]{1,0:T(8,128)S(1)} %collective-permute-done.1), kind=kOutput, calls=%fused_computation.21 | convolution fusion | flops 453181440 | bytes 1769472 | tf_op jit(solution)/shard_map/ij,iw->jw/dot_general | solution.py:37
  34.6 0.1 collective-permute-start.3
  34.7 0.7 %slice_reduce_fusion.1 = s32[384]{0:T(512)S(1)} fusion(s32[4,5,384]{2,0,1:T(4,128)} %param.8), kind=kLoop, calls=%fused_computation.70 | loop fusion | bytes 3072 | tf_op jit(solution)/shard_map/slice | solution.py:33
  35.4 0.8 %fusion.15 = f32[384,256]{1,0:T(8,128)S(1)} fusion(f32[384,256]{1,0:T(8,128)S(1)} %collective-permute-done.1, f32[384,384]{1,0:T(8,128)S(1)} %bitcast_multiply_fusion.1, f32[384,256]{1,0:T(8,128)S(1)} %collective-permute-done.2), kind=kOutput, calls=%fused_computation.23 | convolution fusion | flops 453181440 | bytes 1769472 | tf_op jit(solution)/shard_map/dot_general | solution.py:38
  36.2 8.4 %collective-permute-done.3 = f32[384,256]{1,0:T(8,128)S(1)} collective-permute-done((f32[384,256]{1,0:T(8,128)S(1)}, f32[384,256]{1,0:T(8,128)S(1)}, u32[]{:S(2)}, u32[]{:S(2)}) %collective-permute-start.3) | collective-permute-done | bytes 393248 | tf_op jit(solution)/shard_map/ppermute | solution.py:15
  44.6 0.2 mul.115
  44.8 1.7 %bitcast_multiply_fusion = f32[384,384]{1,0:T(8,128)S(1)} fusion(f32[48,8,3,128]{3,2,1,0:T(4,128)S(1)} %bitcast.75, f32[384,256]{1,0:T(8,128)S(1)} %fusion.15, f32[384,256]{1,0:T(8,128)S(1)} %collective-permute-done.3, s32[4,384,384]{2,1,0:T(8,128)S(1)} %copy-done.2, s32[384]{0:T(512)S(1)} %get-tuple-element.20, s32[384]{0:T(512)S(1)} %slice_reduce_fusion.1, ...), kind=kOutput, calls=%fused_computation.32 | convolution fusion | flops 456376320 | bytes 2563584 | tf_op jit(solution)/shard_map/iw,jw->ij/dot_general | solution.py:29
  46.5 1.1 %fusion.12 = f32[384,256]{1,0:T(8,128)S(1)} fusion(f32[384,256]{1,0:T(8,128)S(1)} %collective-permute-done.3, f32[384,384]{1,0:T(8,128)S(1)} %bitcast_multiply_fusion, f32[384,256]{1,0:T(8,128)S(1)} %fusion.15), kind=kOutput, calls=%fused_computation.17 | convolution fusion | flops 453181440 | bytes 1769472 | tf_op jit(solution)/shard_map/ij,iw->jw/dot_general | solution.py:37
  47.6 0.1 collective-permute-start.4
  47.7 1.5 %fusion.13 = f32[384,256]{1,0:T(8,128)} fusion(f32[384,256]{1,0:T(8,128)S(1)} %fusion.15, f32[384,384]{1,0:T(8,128)S(1)} %bitcast_multiply_fusion, f32[384,256]{1,0:T(8,128)S(1)} %collective-permute-done.3), kind=kOutput, calls=%fused_computation.19 | convolution fusion | flops 453181440 | bytes 1769472 | tf_op jit(solution)/shard_map/dot_general | solution.py:38
  49.2 8.3 %collective-permute-done.4 = f32[384,256]{1,0:T(8,128)S(1)} collective-permute-done((f32[384,256]{1,0:T(8,128)S(1)}, f32[384,256]{1,0:T(8,128)S(1)}, u32[]{:S(2)}, u32[]{:S(2)}) %collective-permute-start.4) | collective-permute-done | bytes 393248 | tf_op jit(solution)/shard_map/ppermute | solution.py:15
  57.5 0.7 %copy.24 = f32[384,256]{1,0:T(8,128)} copy(f32[384,256]{1,0:T(8,128)S(1)} %collective-permute-done.4) | data formatting | bytes 786432
  (2 shorter events, 0.0 us)
Async XLA Ops:
  2.7 2.4 %copy-start = (f32[384,256]{1,0:T(8,128)S(1)}, f32[384,256]{1,0:T(8,128)}, u32[]{:S(2)}) copy-start(f32[384,256]{1,0:T(8,128)} %param.5) | copy-start | bytes 1179652
  2.7 2.4 %copy-start.1 = (f32[384,256]{1,0:T(8,128)S(1)}, f32[384,256]{1,0:T(8,128)}, u32[]{:S(2)}) copy-start(f32[384,256]{1,0:T(8,128)} %param.6) | copy-start | bytes 1179652
  5.1 12.3 %copy-start.2 = (s32[4,384,384]{2,1,0:T(8,128)S(1)}, s32[4,384,384]{2,1,0:T(8,128)}, u32[]{:S(2)}) copy-start(s32[4,384,384]{2,1,0:T(8,128)} %param.7) | copy-start | bytes 7077892
  6.3 11.0 %collective-permute-start = (f32[384,256]{1,0:T(8,128)S(1)}, f32[384,256]{1,0:T(8,128)S(1)}, u32[]{:S(2)}, u32[]{:S(2)}) collective-permute-start(f32[384,256]{1,0:T(8,128)S(1)} %fusion.18), channel_id=1, source_target_pairs={{0,1},{1,2},{2,3},{3,4},{4,5},{5,6},{6,7},{7,8},{8,9},{9,10},{10,1... | collective-permute-start | bytes 1179656 | tf_op jit(solution)/shard_map/ppermute | solution.py:15
  20.3 10.0 %collective-permute-start.2 = (f32[384,256]{1,0:T(8,128)S(1)}, f32[384,256]{1,0:T(8,128)S(1)}, u32[]{:S(2)}, u32[]{:S(2)}) collective-permute-start(f32[384,256]{1,0:T(8,128)S(1)} %fusion.16), channel_id=1, source_target_pairs={{0,1},{1,2},{2,3},{3,4},{4,5},{5,6},{6,7},{7,8},{8,9},{9,10},{10,1... | collective-permute-start | bytes 1179656 | tf_op jit(solution)/shard_map/ppermute | solution.py:15
  21.2 10.4 %collective-permute-start.1 = (f32[384,256]{1,0:T(8,128)S(1)}, f32[384,256]{1,0:T(8,128)S(1)}, u32[]{:S(2)}, u32[]{:S(2)}) collective-permute-start(f32[384,256]{1,0:T(8,128)S(1)} %fusion.17), channel_id=1, source_target_pairs={{0,16},{16,0},{1,17},{17,1},{2,18},{18,2},{3,19},{19,3},{4,20},{20... | collective-permute-start | bytes 1179656 | tf_op jit(solution)/shard_map/ppermute | solution.py:19
  34.6 10.0 %collective-permute-start.3 = (f32[384,256]{1,0:T(8,128)S(1)}, f32[384,256]{1,0:T(8,128)S(1)}, u32[]{:S(2)}, u32[]{:S(2)}) collective-permute-start(f32[384,256]{1,0:T(8,128)S(1)} %fusion.14), channel_id=1, source_target_pairs={{0,1},{1,2},{2,3},{3,4},{4,5},{5,6},{6,7},{7,8},{8,9},{9,10},{10,1... | collective-permute-start | bytes 1179656 | tf_op jit(solution)/shard_map/ppermute | solution.py:15
  47.6 10.0 %collective-permute-start.4 = (f32[384,256]{1,0:T(8,128)S(1)}, f32[384,256]{1,0:T(8,128)S(1)}, u32[]{:S(2)}, u32[]{:S(2)}) collective-permute-start(f32[384,256]{1,0:T(8,128)S(1)} %fusion.12), channel_id=1, source_target_pairs={{0,1},{1,2},{2,3},{3,4},{4,5},{5,6},{6,7},{7,8},{8,9},{9,10},{10,1... | collective-permute-start | bytes 1179656 | tf_op jit(solution)/shard_map/ppermute | solution.py:15
where the time goes:
time: 58.6 us; the launch traced here: 58.3 us
  waiting for transfers between devices  34.8 us (59%)
  matrix products  16 us (27%)
  local copies, waits for them, and re-layouts  3.17 us (5%)
  starting transfers between devices  2.67 us (5%)
  other arithmetic  0.85 us (1%)
  between operations  0.82 us (1%)
    ppermute x4, waiting for transfers between devices, passed_along(): return lax.ppermute(value, axis, pairs)  33.4 us
    dot_general x4, matrix products, one_pass(): scores = jnp.einsum('iw,jw->ij', vert, ctx, precision=highest)  7.51 us
    dot_general x4, matrix products, one_pass(): new_ctx = ctx + eta * jnp.einsum('ij,iw->jw', coef, vert, precision=highest)  4.52 us
    dot_general x4, matrix products, one_pass(): new_vert = vert + eta * jnp.dot(coef, ctx, precision=highest)  3.94 us
    ppermute x1, starting transfers between devices, from_partner(): lax.ppermute(value, axis, [(i, i ^ 1 << stride) for i in range(lax.axis_s...  1.99 us
    slice x2, local copies, waits for them, and re-layouts, one_pass(): neg_rows[sample][:, None] == columns  1.73 us
    ppermute x1, waiting for transfers between devices, from_partner(): lax.ppermute(value, axis, [(i, i ^ 1 << stride) for i in range(lax.axis_s...  1.38 us
  transfers between devices with their start and end apart: 5, of which 5 were waited for; matrix products, arithmetic and copies ran while one was open for 8% of the time, Pallas kernels for 0%

commit v1 on v0

v1 whole, which is shorter than its diff:
```python
import functools
import math

import jax
import jax.numpy as jnp
from jax import lax
from jax.experimental import pallas as pl
from jax.experimental.pallas import tpu as pltpu
from jax.sharding import PartitionSpec as P

ROUNDS = 2
ROUND_PASSES = 2
PASSES = ROUNDS * ROUND_PASSES
F32 = jnp.float32
BF16 = jnp.bfloat16
MESH = pl.DeviceIdType.MESH


def halves(x):
    hi = x.astype(BF16)
    return hi, (x - hi.astype(F32)).astype(BF16)


def dot3(a, b, dims):
    def one(x, y):
        return lax.dot_general(x, y, (dims, ((), ())), preferred_element_type=F32)

    return one(a[0], b[0]) + (one(a[0], b[1]) + one(a[1], b[0]))


NN = ((1,), (0,))
NT = ((1,), (1,))
TN = ((0,), (0,))


def kernel(
    tiles, v_hbm, c_hbm, cnt_hbm, neg_ref, mask_ref, vout, cout,
    vbuf, cbuf, cnt, pbuf, qbuf, vsplit, csplit,
    in_sem, cnt_sem, csend, crecv, vsend, vrecv,
):
    rows = v_hbm.shape[0]
    tile = rows // tiles
    eta = 0.25 / math.sqrt(rows)
    negs = neg_ref.shape[1]
    grp, blk = lax.axis_index("grp"), lax.axis_index("blk")
    n = lax.axis_size("blk")
    right = (grp, lax.rem(blk + 1, n))
    left = (grp, lax.rem(blk + n - 1, n))
    partner = (grp + 1 - 2 * lax.rem(grp, 2), blk)

    barrier = pltpu.get_barrier_semaphore()
    for other in (left, partner):
        pl.semaphore_signal(barrier, inc=1, device_id=other, device_id_type=MESH)

    load_cnt = [pltpu.make_async_copy(cnt_hbm.at[q], cnt.at[q], cnt_sem.at[q]) for q in range(PASSES)]
    load_v = pltpu.make_async_copy(v_hbm, vbuf.at[0], in_sem.at[0])
    load_c = pltpu.make_async_copy(c_hbm, cbuf.at[0], in_sem.at[1])
    load_cnt[0].start()
    load_v.start()
    load_c.start()
    for q in range(1, PASSES):
        load_cnt[q].start()

    def span(k):
        return pl.ds(k * tile, tile)

    def prepare(q):
        load_cnt[q].wait()
        picked = neg_ref[q].astype(F32)
        picked = jnp.concatenate([picked, jnp.full((8 - negs % 8, rows), -1.0, F32)], axis=0).T
        for i in range(tiles):
            mine = picked[i * tile : (i + 1) * tile]
            for j in range(tiles):
                columns = (lax.broadcasted_iota(jnp.int32, (tile, tile), 1) + j * tile).astype(F32)
                seen = jnp.zeros((tile, tile), F32)
                for s in range(negs):
                    seen = seen + jnp.where(mine[:, s : s + 1] == columns, 1.0, 0.0)
                scale = mask_ref[q, i, j].astype(F32) * (0.5 * eta)
                pos = cnt[q, span(i), span(j)].astype(F32)
                pbuf[q, span(i), span(j)] = (pos - seen) * scale
                qbuf[q, span(i), span(j)] = (pos + seen) * scale

    def c_copy(q, k):
        target = cbuf.at[q + 1] if q < PASSES - 1 else cout
        source = cnew(q).at[span(k)]
        return pltpu.make_async_remote_copy(
            src_ref=source, dst_ref=target.at[span(k)], send_sem=csend.at[q, k],
            recv_sem=crecv.at[q, k], device_id=right, device_id_type=MESH,
        )

    def cnew(q):
        return cbuf.at[PASSES + q]

    def v_copy(k):
        return pltpu.make_async_remote_copy(
            src_ref=vbuf.at[2, span(k)], dst_ref=vbuf.at[3, span(k)], send_sem=vsend.at[k],
            recv_sem=vrecv.at[k], device_id=partner, device_id_type=MESH,
        )

    def by_context(q, vin, vnext):
        vhi, vlo = halves(vin[...])
        vsplit[0] = vhi
        vsplit[1] = vlo
        for j in range(tiles):
            if q > 0:
                c_copy(q - 1, j).wait_recv()
            ctx = cbuf[q, span(j)]
            chl = halves(ctx)
            vhl = (vsplit[0], vsplit[1])
            scores = dot3(vhl, chl, NT)
            coef = halves(pbuf[q, :, span(j)] - qbuf[q, :, span(j)] * jnp.tanh(0.5 * scores))
            cnew(q)[span(j)] = ctx + dot3(coef, vhl, TN)
            if q == 0 and j == 0:
                pl.semaphore_wait(barrier, 2)
            c_copy(q, j).start()
            base = vin[...] if j == 0 else vnext[...]
            vnext[...] = base + dot3(coef, chl, NN)

    def by_vertex(q, vin, vnext):
        for j in range(tiles):
            c_copy(q - 1, j).wait_recv()
        chi, clo = halves(cbuf[q])
        csplit[0] = chi
        csplit[1] = clo
        for i in range(tiles):
            v_copy(i).wait_recv()
            vert = vin[span(i)]
            vhl = halves(vert)
            chl = (csplit[0], csplit[1])
            scores = dot3(vhl, chl, NT)
            coef = halves(pbuf[q, span(i)] - qbuf[q, span(i)] * jnp.tanh(0.5 * scores))
            base = cbuf[q] if i == 0 else cnew(q)[...]
            cnew(q)[...] = base + dot3(coef, vhl, TN)
            if i == tiles - 1:
                for j in range(tiles):
                    c_copy(q, j).start()
            vnext[span(i)] = vert + dot3(coef, chl, NN)

    prepare(0)
    load_v.wait()
    load_c.wait()
    by_context(0, vbuf.at[0], vbuf.at[1])
    prepare(1)
    by_context(1, vbuf.at[1], vbuf.at[2])
    for k in range(tiles):
        v_copy(k).start()
    prepare(2)
    prepare(3)
    by_vertex(2, vbuf.at[3], vbuf.at[4])
    by_context(3, vbuf.at[4], vout)
    for j in range(tiles):
        c_copy(PASSES - 1, j).wait_recv()
    for k in range(tiles):
        v_copy(k).wait_send()
        for q in range(PASSES):
            c_copy(q, k).wait_send()


def on_device(vertex_embed, context_embed, counts, negatives, masks):
    rows, width = vertex_embed.shape
    tiles = masks.shape[1]
    state = jax.ShapeDtypeStruct((rows, width), F32)
    hbm = pl.BlockSpec(memory_space=pl.ANY)
    vmem = pl.BlockSpec(memory_space=pltpu.VMEM)
    return pl.pallas_call(
        functools.partial(kernel, tiles),
        out_shape=(state, state),
        in_specs=[hbm, hbm, hbm, vmem, pl.BlockSpec(memory_space=pltpu.SMEM)],
        out_specs=(vmem, vmem),
        scratch_shapes=[
            pltpu.VMEM((5, rows, width), F32),
            pltpu.VMEM((2 * PASSES, rows, width), F32),
            pltpu.VMEM((PASSES, rows, rows), jnp.int32),
            pltpu.VMEM((PASSES, rows, rows), F32),
            pltpu.VMEM((PASSES, rows, rows), F32),
            pltpu.VMEM((2, rows, width), BF16),
            pltpu.VMEM((2, rows, width), BF16),
            pltpu.SemaphoreType.DMA((2,)),
            pltpu.SemaphoreType.DMA((PASSES,)),
            pltpu.SemaphoreType.DMA((PASSES, tiles)),
            pltpu.SemaphoreType.DMA((PASSES, tiles)),
            pltpu.SemaphoreType.DMA((tiles,)),
            pltpu.SemaphoreType.DMA((tiles,)),
        ],
        compiler_params=pltpu.CompilerParams(
            collective_id=0, has_side_effects=True, vmem_limit_bytes=40 * 1024 * 1024
        ),
    )(vertex_embed, context_embed, counts, negatives, masks)


def solution(mesh):
    placed = (
        P(("grp", "blk"), None),
        P(("grp", "blk"), None),
        P(None, ("grp", "blk"), None),
        P(None, None, ("grp", "blk")),
        P(None, ("grp", "blk"), None),
    )
    return jax.shard_map(
        on_device,
        mesh=mesh,
        in_specs=placed,
        out_specs=(P(("grp", "blk"), None), P(("grp", "blk"), None)),
        check_vma=False,
    )
```

time: 58.6 us -> 40.5 us (0.69)
  waiting for transfers between devices: 34.8 us -> 0 us
  Pallas kernels: 0 us -> 33 us
  matrix products: 16 us -> 0 us
  local copies, waits for them, and re-layouts: 3.17 us -> 6.6 us
  starting transfers between devices: 2.67 us -> 0 us
  other arithmetic: 0.85 us -> 0 us
    ppermute x5 -> x0, waiting for transfers between devices: 34.8 us -> none  [the longest x4 33.4 us: passed_along(): return lax.ppermute(value, axis, pairs)]
    pallas_call x0 -> x1, Pallas kernels: none -> 33 us  [on_device(): pl.pallas_call(functools.partial(kernel, tiles), out_shape=(state, state)...]
    dot_general x12 -> x0, matrix products: 16 us -> none  [the longest x4 7.51 us: one_pass(): scores = jnp.einsum('iw,jw->ij', vert, ctx, precision=highest)]
    unnamed x9 -> x10, local copies, waits for them, and re-layouts: 0.77 us -> 6.6 us
    ppermute x5 -> x0, starting transfers between devices: 2.67 us -> none  [the longest x1 1.99 us: from_partner(): lax.ppermute(value, axis, [(i, i ^ 1 << stride) for i in range(lax.axis_s...]
    slice x2 -> x0, local copies, waits for them, and re-layouts: 1.73 us -> none  [one_pass(): neg_rows[sample][:, None] == columns]
    convert_element_type x1 -> x0, other arithmetic: 0.85 us -> none  [one_pass(): gate = tile_mask.astype(jnp.float32)[:, None, :, None]]
    mul x4 -> x0, local copies, waits for them, and re-layouts: 0.67 us -> none  [one_pass(): coef = (coef.reshape(tiles, tile, tiles, tile) * gate).reshape(rows, rows)]
  transfers between devices with their start and end apart: 5 -> 0, of which waited for: 5 -> 0; matrix products, arithmetic and copies ran while one was open for 8% -> 0% of each run, Pallas kernels for 0% -> 0%
where the time goes in v1:
time: 40.5 us; the launch traced here: 40.2 us
  Pallas kernels  33 us (81%)
  local copies, waits for them, and re-layouts  6.6 us (16%)
  between operations  0.64 us (2%)
    pallas_call x1, Pallas kernels, on_device(): pl.pallas_call(functools.partial(kernel, tiles), out_shape=(state, state)...  33 us
    unnamed x10, local copies, waits for them, and re-layouts  6.6 us

profile of v1, /device:TPU:0, one launch (start us, length us, event | category | flops | bytes accessed | tf_op | source)
XLA Modules:
  0.0 40.2 jit_solution(7581341085529890876)
XLA Ops:
  0.6 0.7 %copy.8.mask_ref = s32[4,3,3]{2,1,0:T(4,128)S(1)} copy(s32[4,3,3]{2,0,1:T(4,128)} %param.9) | data formatting | bytes 288 | tf_op args[4]
  1.3 0.8 %copy.7.neg_ref = s32[4,5,384]{2,1,0:T(8,128)S(1)} copy(s32[4,5,384]{2,0,1:T(4,128)} %param.8) | data formatting | bytes 61440 | tf_op args[3]
  2.1 0.0 copy-start
  2.1 1.7 %copy-done = s32[4,384,384]{2,1,0:T(8,128)S(1)} copy-done((s32[4,384,384]{2,1,0:T(8,128)S(1)}, s32[4,384,384]{2,1,0:T(8,128)}, u32[]{:S(2)}) %copy-start) | copy-done | bytes 2359320
  3.7 0.0 copy-start.1
  3.8 1.0 %copy-done.1 = f32[384,256]{1,0:T(8,128)S(1)} copy-done((f32[384,256]{1,0:T(8,128)S(1)}, f32[384,256]{1,0:T(8,128)}, u32[]{:S(2)}) %copy-start.1) | copy-done | bytes 393240
  4.7 0.0 copy-start.2
  4.7 1.0 %copy-done.2 = f32[384,256]{1,0:T(8,128)S(1)} copy-done((f32[384,256]{1,0:T(8,128)S(1)}, f32[384,256]{1,0:T(8,128)}, u32[]{:S(2)}) %copy-start.2) | copy-done | bytes 393240
  5.7 33.0 %shard_map.68 = (f32[384,256]{1,0:T(8,128)S(1)}, f32[384,256]{1,0:T(8,128)S(1)}) custom-call(f32[384,256]{1,0:T(8,128)S(1)} %copy-done.1, f32[384,256]{1,0:T(8,128)S(1)} %copy-done.2, s32[4,384,384]{2,1,0:T(8,128)S(1)} %copy-done, s32[4,5,384]{2,1,0:T(8,128)S(1)} %copy.7.neg_ref, s32[4,3,3]{2,1,0:T(4,128)S(1)} %copy.8.mask_ref), custom_call_target="tpu_custom_call" | custom-call | tf_op jit(solution)/shard_map/pallas_call | solution.py:165
  38.7 0.7 %copy.11 = f32[384,256]{1,0:T(8,128)} copy(f32[384,256]{1,0:T(8,128)S(1)} %get-tuple-element.4) | data formatting | bytes 786432
  39.5 0.7 %copy.12 = f32[384,256]{1,0:T(8,128)} copy(f32[384,256]{1,0:T(8,128)S(1)} %get-tuple-element.5) | data formatting | bytes 786432
Async XLA Ops:
  2.1 1.7 %copy-start = (s32[4,384,384]{2,1,0:T(8,128)S(1)}, s32[4,384,384]{2,1,0:T(8,128)}, u32[]{:S(2)}) copy-start(s32[4,384,384]{2,1,0:T(8,128)} %cnt_hbm.1) | copy-start | bytes 7077892
  3.7 1.0 %copy-start.1 = (f32[384,256]{1,0:T(8,128)S(1)}, f32[384,256]{1,0:T(8,128)}, u32[]{:S(2)}) copy-start(f32[384,256]{1,0:T(8,128)} %v_hbm.1) | copy-start | bytes 1179652
  4.7 1.0 %copy-start.2 = (f32[384,256]{1,0:T(8,128)S(1)}, f32[384,256]{1,0:T(8,128)}, u32[]{:S(2)}) copy-start(f32[384,256]{1,0:T(8,128)} %c_hbm.1) | copy-start | bytes 1179652

commit v2 on v1

--- a/solution.py
+++ b/solution.py
@@ -22,10 +22,10 @@
 
 
 def dot3(a, b, dims):
-    def one(x, y):
-        return lax.dot_general(x, y, (dims, ((), ())), preferred_element_type=F32)
-
-    return one(a[0], b[0]) + (one(a[0], b[1]) + one(a[1], b[0]))
+    left, right = dims[0][0], dims[1][0]
+    stacked_a = jnp.concatenate([a[0], a[0], a[1]], axis=left)
+    stacked_b = jnp.concatenate([b[0], b[1], b[0]], axis=right)
+    return lax.dot_general(stacked_a, stacked_b, (dims, ((), ())), preferred_element_type=F32)
 
 
 NN = ((1,), (0,))
@@ -41,7 +41,7 @@
     rows = v_hbm.shape[0]
     tile = rows // tiles
     eta = 0.25 / math.sqrt(rows)
-    negs = neg_ref.shape[1]
+    negs = neg_ref.shape[0]
     grp, blk = lax.axis_index("grp"), lax.axis_index("blk")
     n = lax.axis_size("blk")
     right = (grp, lax.rem(blk + 1, n))
@@ -58,15 +58,27 @@
     load_cnt[0].start()
     load_v.start()
     load_c.start()
-    for q in range(1, PASSES):
-        load_cnt[q].start()
 
     def span(k):
         return pl.ds(k * tile, tile)
 
-    def prepare(q):
+    def prepare_by_context(q):
         load_cnt[q].wait()
-        picked = neg_ref[q].astype(F32)
+        for j in range(tiles):
+            column = lax.broadcasted_iota(jnp.int32, (tile, rows), 0) + j * tile
+            seen = jnp.zeros((tile, rows), F32)
+            for s in range(negs):
+                seen = seen + jnp.where(neg_ref[s, q : q + 1, :] == column, 1.0, 0.0)
+            for i in range(tiles):
+                scale = mask_ref[i, q, j].astype(F32) * (0.5 * eta)
+                pos = cnt[q, span(i), span(j)].astype(F32).T
+                there = seen[:, i * tile : (i + 1) * tile]
+                pbuf[q, span(j), span(i)] = (pos - there) * scale
+                qbuf[q, span(j), span(i)] = (pos + there) * scale
+
+    def prepare_by_vertex(q):
+        load_cnt[q].wait()
+        picked = neg_ref[:, q, :].astype(F32)
         picked = jnp.concatenate([picked, jnp.full((8 - negs % 8, rows), -1.0, F32)], axis=0).T
         for i in range(tiles):
             mine = picked[i * tile : (i + 1) * tile]
@@ -75,7 +87,7 @@
                 seen = jnp.zeros((tile, tile), F32)
                 for s in range(negs):
                     seen = seen + jnp.where(mine[:, s : s + 1] == columns, 1.0, 0.0)
-                scale = mask_ref[q, i, j].astype(F32) * (0.5 * eta)
+                scale = mask_ref[i, q, j].astype(F32) * (0.5 * eta)
                 pos = cnt[q, span(i), span(j)].astype(F32)
                 pbuf[q, span(i), span(j)] = (pos - seen) * scale
                 qbuf[q, span(i), span(j)] = (pos + seen) * scale
@@ -107,14 +119,14 @@
             ctx = cbuf[q, span(j)]
             chl = halves(ctx)
             vhl = (vsplit[0], vsplit[1])
-            scores = dot3(vhl, chl, NT)
-            coef = halves(pbuf[q, :, span(j)] - qbuf[q, :, span(j)] * jnp.tanh(0.5 * scores))
-            cnew(q)[span(j)] = ctx + dot3(coef, vhl, TN)
+            scores = dot3(chl, vhl, NT)
+            coef = halves(pbuf[q, span(j)] - qbuf[q, span(j)] * jnp.tanh(0.5 * scores))
+            cnew(q)[span(j)] = ctx + dot3(coef, vhl, NN)
             if q == 0 and j == 0:
                 pl.semaphore_wait(barrier, 2)
             c_copy(q, j).start()
             base = vin[...] if j == 0 else vnext[...]
-            vnext[...] = base + dot3(coef, chl, NN)
+            vnext[...] = base + dot3(coef, chl, TN)
 
     def by_vertex(q, vin, vnext):
         for j in range(tiles):
@@ -136,16 +148,18 @@
                     c_copy(q, j).start()
             vnext[span(i)] = vert + dot3(coef, chl, NN)
 
-    prepare(0)
+    prepare_by_context(0)
     load_v.wait()
     load_c.wait()
+    for q in range(1, PASSES):
+        load_cnt[q].start()
     by_context(0, vbuf.at[0], vbuf.at[1])
-    prepare(1)
+    prepare_by_context(1)
     by_context(1, vbuf.at[1], vbuf.at[2])
     for k in range(tiles):
         v_copy(k).start()
-    prepare(2)
-    prepare(3)
+    prepare_by_vertex(2)
+    prepare_by_context(3)
     by_vertex(2, vbuf.at[3], vbuf.at[4])
     by_context(3, vbuf.at[4], vout)
     for j in range(tiles):
@@ -160,7 +174,7 @@
     rows, width = vertex_embed.shape
     tiles = masks.shape[1]
     state = jax.ShapeDtypeStruct((rows, width), F32)
-    hbm = pl.BlockSpec(memory_space=pl.ANY)
+    hbm = pl.BlockSpec(memory_space=pltpu.HBM)
     vmem = pl.BlockSpec(memory_space=pltpu.VMEM)
     return pl.pallas_call(
         functools.partial(kernel, tiles),
@@ -183,9 +197,9 @@
             pltpu.SemaphoreType.DMA((tiles,)),
         ],
         compiler_params=pltpu.CompilerParams(
-            collective_id=0, has_side_effects=True, vmem_limit_bytes=40 * 1024 * 1024
+            collective_id=0, has_side_effects=True, vmem_limit_bytes=60 * 1024 * 1024
         ),
-    )(vertex_embed, context_embed, counts, negatives, masks)
+    )(vertex_embed, context_embed, counts, negatives.transpose(1, 0, 2), masks.transpose(1, 0, 2))
 
 
 def solution(mesh):

time: 40.5 us -> 37.4 us (0.923)
  local copies, waits for them, and re-layouts: 6.6 us -> 3.53 us
    unnamed x10 -> x2, local copies, waits for them, and re-layouts: 6.6 us -> 3.53 us
where the time goes in v2:
time: 37.4 us; the launch traced here: 37.1 us
  Pallas kernels  32.9 us (88%)
  local copies, waits for them, and re-layouts  3.53 us (9%)
  between operations  0.64 us (2%)
    pallas_call x1, Pallas kernels, on_device(): pl.pallas_call(functools.partial(kernel, tiles), out_shape=(state, state)...  32.9 us
    unnamed x2, local copies, waits for them, and re-layouts  3.53 us

profile of v2, /device:TPU:0, one launch (start us, length us, event | category | flops | bytes accessed | tf_op | source)
XLA Modules:
  0.0 37.1 jit_solution(12512021849945874958)
XLA Ops:
  0.6 32.9 %shard_map.68 = (f32[384,256]{1,0:T(8,128)}, f32[384,256]{1,0:T(8,128)}) custom-call(f32[384,256]{1,0:T(8,128)} %v_hbm.1, f32[384,256]{1,0:T(8,128)} %c_hbm.1, s32[4,384,384]{2,1,0:T(8,128)} %cnt_hbm.1, s32[5,4,384]{2,1,0:T(4,128)} %bitcast.2, s32[3,4,3]{2,1,0:T(4,128)} %bitcast.3), custom_call_target="tpu_custom_call" | custom-call | tf_op jit(solution)/shard_map/pallas_call | solution.py:179
  33.6 1.8 %copy.9 = f32[384,256]{1,0:T(8,128)} copy(f32[384,256]{1,0:T(8,128)} %get-tuple-element.4) | data formatting | bytes 786432
  35.3 1.8 %copy.10 = f32[384,256]{1,0:T(8,128)} copy(f32[384,256]{1,0:T(8,128)} %get-tuple-element.5) | data formatting | bytes 786432

commit v3 on v2

--- a/solution.py
+++ b/solution.py
@@ -135,18 +135,23 @@
         csplit[0] = chi
         csplit[1] = clo
         for i in range(tiles):
-            v_copy(i).wait_recv()
+            if q == ROUND_PASSES:
+                v_copy(i).wait_recv()
             vert = vin[span(i)]
             vhl = halves(vert)
             chl = (csplit[0], csplit[1])
             scores = dot3(vhl, chl, NT)
             coef = halves(pbuf[q, span(i)] - qbuf[q, span(i)] * jnp.tanh(0.5 * scores))
+            if q == ROUND_PASSES - 1:
+                vnext[span(i)] = vert + dot3(coef, chl, NN)
+                v_copy(i).start()
             base = cbuf[q] if i == 0 else cnew(q)[...]
             cnew(q)[...] = base + dot3(coef, vhl, TN)
             if i == tiles - 1:
                 for j in range(tiles):
                     c_copy(q, j).start()
-            vnext[span(i)] = vert + dot3(coef, chl, NN)
+            if q != ROUND_PASSES - 1:
+                vnext[span(i)] = vert + dot3(coef, chl, NN)
 
     prepare_by_context(0)
     load_v.wait()
@@ -154,16 +159,17 @@
     for q in range(1, PASSES):
         load_cnt[q].start()
     by_context(0, vbuf.at[0], vbuf.at[1])
-    prepare_by_context(1)
-    by_context(1, vbuf.at[1], vbuf.at[2])
-    for k in range(tiles):
-        v_copy(k).start()
+    prepare_by_vertex(1)
+    by_vertex(1, vbuf.at[1], vbuf.at[2])
     prepare_by_vertex(2)
     prepare_by_context(3)
     by_vertex(2, vbuf.at[3], vbuf.at[4])
-    by_context(3, vbuf.at[4], vout)
+    by_context(3, vbuf.at[4], vbuf.at[5])
+    store_v = pltpu.make_async_copy(vbuf.at[5], vout, in_sem.at[0])
+    store_v.start()
     for j in range(tiles):
         c_copy(PASSES - 1, j).wait_recv()
+    store_v.wait()
     for k in range(tiles):
         v_copy(k).wait_send()
         for q in range(PASSES):
@@ -180,9 +186,9 @@
         functools.partial(kernel, tiles),
         out_shape=(state, state),
         in_specs=[hbm, hbm, hbm, vmem, pl.BlockSpec(memory_space=pltpu.SMEM)],
-        out_specs=(vmem, vmem),
+        out_specs=(hbm, hbm),
         scratch_shapes=[
-            pltpu.VMEM((5, rows, width), F32),
+            pltpu.VMEM((6, rows, width), F32),
             pltpu.VMEM((2 * PASSES, rows, width), F32),
             pltpu.VMEM((PASSES, rows, rows), jnp.int32),
             pltpu.VMEM((PASSES, rows, rows), F32),

time: 37.4 us -> 36 us (0.963)
  Pallas kernels: 32.9 us -> 31.5 us
    pallas_call x1, Pallas kernels: 32.9 us -> 31.5 us  [on_device(): pl.pallas_call(functools.partial(kernel, tiles), out_shape=(state, state)...]
where the time goes in v3:
time: 36 us; the launch traced here: 35.7 us
  Pallas kernels  31.5 us (88%)
  local copies, waits for them, and re-layouts  3.53 us (10%)
  between operations  0.64 us (2%)
    pallas_call x1, Pallas kernels, on_device(): pl.pallas_call(functools.partial(kernel, tiles), out_shape=(state, state)...  31.5 us
    unnamed x2, local copies, waits for them, and re-layouts  3.53 us

profile of v3, /device:TPU:0, one launch (start us, length us, event | category | flops | bytes accessed | tf_op | source)
XLA Modules:
  0.0 35.7 jit_solution(1503017811209937632)
XLA Ops:
  0.6 31.5 %shard_map.68 = (f32[384,256]{1,0:T(8,128)}, f32[384,256]{1,0:T(8,128)}) custom-call(f32[384,256]{1,0:T(8,128)} %v_hbm.1, f32[384,256]{1,0:T(8,128)} %c_hbm.1, s32[4,384,384]{2,1,0:T(8,128)} %cnt_hbm.1, s32[5,4,384]{2,1,0:T(4,128)} %bitcast.2, s32[3,4,3]{2,1,0:T(4,128)} %bitcast.3), custom_call_target="tpu_custom_call" | custom-call | tf_op jit(solution)/shard_map/pallas_call | solution.py:185
  32.1 1.8 %copy.9 = f32[384,256]{1,0:T(8,128)} copy(f32[384,256]{1,0:T(8,128)} %get-tuple-element.4) | data formatting | bytes 786432
  33.9 1.8 %copy.10 = f32[384,256]{1,0:T(8,128)} copy(f32[384,256]{1,0:T(8,128)} %get-tuple-element.5) | data formatting | bytes 786432
